TPU v7x, 32 devices: a whole 2x2x4 slice. The times are simulated.
32 devices in a mesh: groups: 2 (over y), tiles: 4 (over z), cols: 2 (over core), dates: 2 (over x).
Axes of the slice: x: 2, y: 2, z: 4, core: 2. Of those that a mesh axis runs over, the one named last changes fastest.
Arguments:
- imagery: bfloat16 [8, 4, 432, 4096], P(('groups', 'tiles'), 'cols', 'dates'), parts along dimension 0, may hold values from -6 to 6
- pixel_mask: int32 [8, 4, 4096], P(('groups', 'tiles'), ('cols', 'dates')), parts along dimension 0, may hold values 0 or 1
- point_pixel: int32 [8, 4, 4096], P(('groups', 'tiles'), ('cols', 'dates')), parts along dimension 0, may hold values from 0 to 4095
- point_yield: float32 [8, 4, 4096], P(('groups', 'tiles'), ('cols', 'dates')), parts along dimension 0, may hold values from -6 to 6
Outputs:
- prediction: float32 [8, 4, 4096], P(('groups', 'tiles'), ('cols', 'dates')), parts along dimension 0
- distance: float32 [8, 4, 4096], P(('groups', 'tiles'), ('cols', 'dates')), parts along dimension 0
- residual: float32 [8, 4, 4096], P(('groups', 'tiles'), ('cols', 'dates')), parts along dimension 0
There are 2 independent parts, one for each index of `groups`. A program takes and returns all parts, laid end to end along the dimension named above; each array names one. Nothing has to cross between parts.
All inputs are finite; a program needn't handle non-finite values. No bound on the sum of `pixel_mask` on one device may be relied on, other than what follows from the above.
Results may differ from a plain program's by a relative error of at most 0.0003.
Values may be sent and summed in bfloat16 or wider, within the bound.
A program may use at most 128 MiB of HBM per device.

v0:
```python
import jax
import jax.numpy as jnp
from jax import lax
from jax.experimental import pallas as pl
from jax.experimental.pallas import tpu as pltpu
from jax.sharding import PartitionSpec as P

ridge_term = 0.05
LANES = 128
CHUNK = 512
F32 = jnp.float32
BF16 = jnp.bfloat16
NT = (((1,), (1,)), ((), ()))


def split3(x):
    a = x.astype(BF16)
    rest = x - a.astype(F32)
    b = rest.astype(BF16)
    c = (rest - b.astype(F32)).astype(BF16)
    return a, b, c


def one_hots(index, rows):
    points = index.shape[1]
    high = lax.broadcasted_iota(jnp.int32, (rows, points), 0) == index // LANES
    low = lax.broadcasted_iota(jnp.int32, (LANES, points), 0) == index % LANES
    return high, low


def segment_kernel(index_ref, yield_ref, mask_ref, weight_ref, product_ref):
    rows = mask_ref.shape[0]
    high, low = one_hots(index_ref[...], rows)
    low = jnp.where(low, 1.0, 0.0).astype(BF16)
    pieces = [jnp.where(high, 1.0, 0.0).astype(BF16)]
    for piece in split3(yield_ref[...]):
        pieces.append(jnp.where(high, piece.astype(F32), 0.0).astype(BF16))
    sums = lax.dot_general(
        jnp.concatenate(pieces, 0), low, NT, preferred_element_type=F32
    )
    counts = sums[:rows]
    totals = sums[rows : 2 * rows] + sums[2 * rows : 3 * rows] + sums[3 * rows :]
    weight = jnp.where(counts > 0, mask_ref[...].astype(F32), 0.0)
    weight_ref[...] = weight
    product_ref[...] = weight * (totals / jnp.maximum(counts, 1.0))


def bands(width):
    blocks, offset = [], 0
    for i in range(pl.cdiv(width, LANES)):
        height = min(LANES, width - i * LANES)
        for j in range(i + 1):
            blocks.append((i, j, height, offset))
            offset += height
    return blocks, offset


def gram_kernel(feats_ref, weight_ref, product_ref, out_ref, acc):
    width, pixels = feats_ref.shape
    acc[...] = jnp.zeros_like(acc)

    def step(c, _):
        at = pl.multiple_of(c * CHUNK, CHUNK)
        feats = feats_ref[:, pl.ds(at, CHUNK)]
        left = []
        for s in range(CHUNK // LANES):
            row = pl.ds(c * (CHUNK // LANES) + s, 1)
            part = feats[:, s * LANES : (s + 1) * LANES]
            scaled = part * weight_ref[row, :].astype(BF16)
            a, b, d = (p.astype(F32) for p in split3(product_ref[row, :]))
            line = lax.broadcasted_iota(jnp.int32, (16, LANES), 0)
            extra = jnp.where(
                line == 0, a, jnp.where(line == 1, b, jnp.where(line == 2, d, 0.0))
            )
            left.append(jnp.concatenate([scaled, extra.astype(BF16)], 0))
        acc[...] += lax.dot_general(
            jnp.concatenate(left, 1), feats, NT, preferred_element_type=F32
        )
        return 0

    lax.fori_loop(0, pixels // CHUNK, step, 0)
    blocks, offset = bands(width)
    out_ref[...] = jnp.zeros_like(out_ref)
    for i, j, height, at in blocks:
        wide = min(LANES, width - j * LANES)
        out_ref[at : at + height, :wide] = acc[
            i * LANES : i * LANES + height, j * LANES : j * LANES + wide
        ]
    moment = acc[width : width + 1] + acc[width + 1 : width + 2]
    moment = moment + acc[width + 2 : width + 3]
    for j in range(pl.cdiv(width, LANES)):
        wide = min(LANES, width - j * LANES)
        out_ref[offset + j : offset + j + 1, :wide] = moment[
            :, j * LANES : j * LANES + wide
        ]


def small_inverse(p):
    n = len(p)
    for k in range(n):
        d = 1.0 / p[k][k]
        row = [d if j == k else p[k][j] * d for j in range(n)]
        new = []
        for i in range(n):
            if i == k:
                new.append(row)
            else:
                new.append(
                    [
                        -p[i][k] * d if j == k else p[i][j] - p[i][k] * row[j]
                        for j in range(n)
                    ]
                )
        p = new
    return p


def block_inverse(block, pivots, group=4):
    tiles = [block[8 * g : 8 * g + 8] for g in range(LANES // 8)]
    lane = lax.broadcasted_iota(jnp.int32, (8, LANES), 1)
    line = lax.broadcasted_iota(jnp.int32, (8, LANES), 0)
    for k in range(0, pivots, group):
        g, r = divmod(k, 8)
        cols = [
            [
                jnp.broadcast_to(t[:, k + j : k + j + 1], (8, LANES))
                for t in tiles
            ]
            for j in range(group)
        ]
        small = [
            [cols[j][g][r + i : r + i + 1] for j in range(group)]
            for i in range(group)
        ]
        small = small_inverse(small)
        rows = []
        for i in range(group):
            old = tiles[g][r + i : r + i + 1]
            old = jnp.where((lane[:1] >= k) & (lane[:1] < k + group), 0.0, old)
            rows.append(jnp.where(lane[:1] == k + i, 1.0, old))
        new_rows = []
        for i in range(group):
            total = small[i][0] * rows[0]
            for j in range(1, group):
                total = total + small[i][j] * rows[j]
            new_rows.append(jnp.broadcast_to(total, (8, LANES)))
        keep = (lane < k) | (lane >= k + group)
        for t in range(LANES // 8):
            value = jnp.where(keep, tiles[t], 0.0)
            for j in range(group):
                value = value - cols[j][t] * new_rows[j]
            if t == g:
                for i in range(group):
                    value = jnp.where(line == r + i, new_rows[i], value)
            tiles[t] = value
    return jnp.concatenate(tiles, 0)


def dot32(a, b):
    return jnp.dot(
        a, b, precision=lax.Precision.HIGHEST, preferred_element_type=F32
    )


def solve_kernel(
    packed_ref,
    feats_ref,
    index_ref,
    yield_ref,
    fitted_ref,
    spread_ref,
    resid_ref,
    system,
    base,
    high_ref,
    low_ref,
    fit,
):
    width, pixels = feats_ref.shape
    count = pl.cdiv(width, LANES)
    size = count * LANES
    blocks, offset = bands(width)
    scale = 1.0 / pixels
    line = lax.broadcasted_iota(jnp.int32, (LANES, LANES), 0)
    lane = lax.broadcasted_iota(jnp.int32, (LANES, LANES), 1)
    for i, j, height, at in blocks:
        value = packed_ref[at : at + height] * scale
        if height < LANES:
            value = jnp.concatenate(
                [value, jnp.zeros((LANES - height, LANES), F32)], 0
            )
        if i == j:
            diagonal = jnp.where(line < height, ridge_term, 1.0)
            value = value + jnp.where(line == lane, diagonal, 0.0)
        system[i * LANES : (i + 1) * LANES, j * LANES : (j + 1) * LANES] = value
        if i != j:
            system[j * LANES : (j + 1) * LANES, i * LANES : (i + 1) * LANES] = value.T

    base[...] = system[...]
    column = lax.broadcasted_iota(jnp.int32, (LANES, size), 1)
    wide_line = lax.broadcasted_iota(jnp.int32, (LANES, size), 0)

    def eliminate(k, pivots):
        at = k * LANES if isinstance(k, int) else pl.multiple_of(k * LANES, LANES)
        here = pl.ds(at, LANES)
        inverse = block_inverse(system[here, here], pivots)
        inside = (column >= at) & (column < at + LANES)
        unit = jnp.where(column == wide_line + at, 1.0, 0.0)
        right = dot32(inverse, jnp.where(inside, unit, system[here, :]))
        left = system[:, here]
        system[:, here] = jnp.zeros_like(left)
        system[...] -= dot32(left, right)
        system[here, :] = right

    full = width // LANES

    def body(k, _):
        eliminate(k, LANES)
        return 0

    lax.fori_loop(0, full, body, 0)
    if width % LANES:
        eliminate(full, width % LANES)

    rhs = jnp.concatenate(
        [packed_ref[offset + j : offset + j + 1] for j in range(count)], 1
    )
    rhs = jnp.broadcast_to(rhs * scale, (8, size))
    beta = dot32(rhs, system[...])
    beta = beta + dot32(rhs - dot32(beta, base[...]), system[...])
    beta = beta[:1, :width]
    inverse = system[:width, :width]
    upper = inverse.astype(BF16)
    a, b, d = (p.astype(F32) for p in split3(beta))
    row16 = lax.broadcasted_iota(jnp.int32, (16, width), 0)
    extra = jnp.where(row16 == 0, a, jnp.where(row16 == 1, b, jnp.where(row16 == 2, d, 0.0)))
    high_ref[...] = jnp.concatenate([upper, extra.astype(BF16)], 0)
    low_ref[...] = (inverse - upper.astype(F32)).astype(BF16)

    def step(c, _):
        at = pl.multiple_of(c * CHUNK, CHUNK)
        feats = feats_ref[:, pl.ds(at, CHUNK)]
        first = jnp.dot(high_ref[...], feats, preferred_element_type=F32)
        second = jnp.dot(low_ref[...], feats, preferred_element_type=F32)
        total = (first[:width] + second) * feats.astype(F32)
        spread_ref[:, pl.ds(at, CHUNK)] = jnp.sum(total, 0, keepdims=True) / width
        fitted = first[width : width + 1] + (
            first[width + 1 : width + 2] + first[width + 2 : width + 3]
        )
        fitted_ref[:, pl.ds(at, CHUNK)] = fitted
        for s in range(CHUNK // LANES):
            fit[pl.ds(c * (CHUNK // LANES) + s, 1), :] = fitted[
                :, s * LANES : (s + 1) * LANES
            ]
        return 0

    lax.fori_loop(0, pixels // CHUNK, step, 0)

    rows = pixels // LANES
    high, low = one_hots(index_ref[...], rows)
    low = jnp.where(low, 1.0, 0.0).astype(BF16)
    table = jnp.concatenate(split3(fit[...]), 0)
    found = jnp.dot(table, low, preferred_element_type=F32)
    found = found[:rows] + (found[rows : 2 * rows] + found[2 * rows :])
    value = jnp.sum(jnp.where(high, found, 0.0), 0, keepdims=True)
    resid_ref[...] = yield_ref[...] - value


PARAMS = pltpu.CompilerParams(vmem_limit_bytes=48 * 1024 * 1024)


def segments(index, yields, mask):
    shape = jax.ShapeDtypeStruct(mask.shape, F32)
    return pl.pallas_call(
        segment_kernel,
        out_shape=(shape, shape),
        compiler_params=PARAMS,
        cost_estimate=pl.CostEstimate(
            flops=2 * 128 * 128 * index.shape[1],
            bytes_accessed=16 * index.shape[1],
            transcendentals=0,
        ),
        name="segments",
    )(index, yields, mask)


def grams(feats, weight, product):
    width, pixels = feats.shape
    rows = bands(width)[1] + 8 * pl.cdiv(pl.cdiv(width, LANES), 8)
    return pl.pallas_call(
        gram_kernel,
        out_shape=jax.ShapeDtypeStruct((rows, LANES), F32),
        scratch_shapes=[pltpu.VMEM((width + 16, width), F32)],
        compiler_params=PARAMS,
        name="grams",
    )(feats, weight, product)


def solves(packed, feats, index, yields):
    width, pixels = feats.shape
    size = pl.cdiv(width, LANES) * LANES
    shape = jax.ShapeDtypeStruct((1, pixels), F32)
    return pl.pallas_call(
        solve_kernel,
        out_shape=(shape, shape, jax.ShapeDtypeStruct(yields.shape, F32)),
        scratch_shapes=[
            pltpu.VMEM((size, size), F32),
            pltpu.VMEM((size, size), F32),
            pltpu.VMEM((width + 16, width), BF16),
            pltpu.VMEM((width, width), BF16),
            pltpu.VMEM((pixels // LANES, LANES), F32),
        ],
        compiler_params=PARAMS,
        name="solves",
    )(packed, feats, index, yields)


def window(x, axis):
    devices = 1
    for name in axis if isinstance(axis, tuple) else (axis,):
        devices *= lax.axis_size(name)
    up = [(i, i + 1) for i in range(devices - 1)]
    down = [(j, i) for i, j in up]
    before = lax.ppermute(x, axis, up)
    after = lax.ppermute(x, axis, down)
    return 0.5 * before + x + 0.5 * after


def on_device(imagery, pixel_mask, point_pixel, point_yield):
    whole = lax.all_to_all(imagery, "dates", split_axis=1, concat_axis=2, tiled=True)
    feats = whole[0, 0]
    pixels = feats.shape[1]
    index = point_pixel[0]
    yields = point_yield[0]
    mask = pixel_mask.reshape(pixels // LANES, LANES)
    weight, product = segments(index, yields, mask)
    packed = grams(feats, weight, product)
    packed = window(packed, "tiles")
    packed = window(packed, ("cols", "dates"))
    fitted, spread, resid = solves(packed, feats, index, yields)
    return (fitted[None], spread[None], resid[None])


def solution(mesh):
    features = P(("groups", "tiles"), "cols", "dates", None)
    points = P(("groups", "tiles"), ("cols", "dates"), None)
    return jax.shard_map(
        on_device,
        mesh=mesh,
        in_specs=(features, points, points, points),
        out_specs=(points, points, points),
        check_vma=False,
    )
```

profile of v0, /device:TPU:0, one launch (start us, length us, event | category | flops | bytes accessed | tf_op | source)
XLA Modules:
  0.0 121.3 jit_solution(11384551889414866206)
XLA Ops:
  0.6 0.0 copy-start
  0.6 4.2 %all-to-all-start = ((bf16[1,2,216,4096]{3,2,0,1:T(8,128)(2,1)}), bf16[1,2,216,4096]{3,2,0,1:T(8,128)(2,1)S(1)}, u32[]{:S(2)}, u32[]{:S(2)}) async-start(bf16[1,2,216,4096]{3,2,0,1:T(8,128)(2,1)} %bitcast.15), calls=%async_computation | async-start | bytes 7077888 | tf_op jit(solution)/shard_map/all_to_all | solution.py:330
  4.9 0.0 copy-done
  4.9 0.0 copy-start.1
  4.9 0.7 copy-done.1
  5.6 0.0 copy-start.7
  5.6 0.7 copy-done.7
  6.3 0.5 segments.1
  6.8 0.0 copy-start.3
  6.8 0.6 copy-done.3
  7.4 0.0 copy-start.5
  7.4 0.6 copy-done.5
  8.0 38.4 %all-to-all-done = bf16[1,2,216,4096]{3,2,0,1:T(8,128)(2,1)S(1)} async-done(((bf16[1,2,216,4096]{3,2,0,1:T(8,128)(2,1)}), bf16[1,2,216,4096]{3,2,0,1:T(8,128)(2,1)S(1)}, u32[]{:S(2)}, u32[]{:S(2)}) %all-to-all-start) | async-done | bytes 3538976 | tf_op jit(solution)/shard_map/all_to_all | solution.py:330
  46.4 0.0 copy-start.4
  46.4 0.7 copy-done.4
  47.1 0.0 copy-start.6
  47.1 0.7 copy-done.6
  47.8 0.0 copy-start.2
  47.9 3.5 %grams.1 = f32[968,128]{1,0:T(8,128)S(1)} custom-call(bf16[432,4096]{1,0:T(8,128)(2,1)S(1)} %bitcast.8, f32[32,128]{1,0:T(8,128)S(1)} %copy-done.4, f32[32,128]{1,0:T(8,128)S(1)} %copy-done.6), custom_call_target="tpu_custom_call" | custom-call | tf_op jit(solution)/shard_map/grams/pallas_call | solution.py:290
  51.4 1.3 %collective-permute-start.1 = (f32[968,128]{1,0:T(8,128)S(1)}, f32[968,128]{1,0:T(8,128)S(1)}, u32[]{:S(2)}, u32[]{:S(2)}) collective-permute-start(f32[968,128]{1,0:T(8,128)S(1)} %grams.1), channel_id=1, source_target_pairs={{4,0},{8,4},{12,8},{5,1},{9,5},{13,9},{6,2},{10,6},{14,10},{7,3},{... | collective-permute-start | bytes 1486856 | tf_op jit(solution)/shard_map/ppermute | solution.py:325
  52.7 4.6 %collective-permute-start = (f32[968,128]{1,0:T(8,128)S(1)}, f32[968,128]{1,0:T(8,128)S(1)}, u32[]{:S(2)}, u32[]{:S(2)}) collective-permute-start(f32[968,128]{1,0:T(8,128)S(1)} %grams.1), channel_id=1, source_target_pairs={{0,4},{4,8},{8,12},{1,5},{5,9},{9,13},{2,6},{6,10},{10,14},{3,7},{... | collective-permute-start | bytes 1486856 | tf_op jit(solution)/shard_map/ppermute | solution.py:324
  57.3 8.5 %collective-permute-done.1 = f32[968,128]{1,0:T(8,128)S(1)} collective-permute-done((f32[968,128]{1,0:T(8,128)S(1)}, f32[968,128]{1,0:T(8,128)S(1)}, u32[]{:S(2)}, u32[]{:S(2)}) %collective-permute-start.1) | collective-permute-done | bytes 495648 | tf_op jit(solution)/shard_map/ppermute | solution.py:325
  65.8 1.2 collective-permute-done
  67.0 0.1 multiply_add_fusion.1
  67.0 1.3 %collective-permute-start.3 = (f32[968,128]{1,0:T(8,128)S(1)}, f32[968,128]{1,0:T(8,128)S(1)}, u32[]{:S(2)}, u32[]{:S(2)}) collective-permute-start(f32[968,128]{1,0:T(8,128)S(1)} %multiply_add_fusion.1), channel_id=1, source_target_pairs={{1,0},{2,1},{3,2},{5,4},{6,5},{7,6},{9,8},{10,9},{11,10},{13,12},{... | collective-permute-start | bytes 1486856 | tf_op jit(solution)/shard_map/ppermute | solution.py:325
  68.3 4.6 %collective-permute-start.2 = (f32[968,128]{1,0:T(8,128)S(1)}, f32[968,128]{1,0:T(8,128)S(1)}, u32[]{:S(2)}, u32[]{:S(2)}) collective-permute-start(f32[968,128]{1,0:T(8,128)S(1)} %multiply_add_fusion.1), channel_id=1, source_target_pairs={{0,1},{1,2},{2,3},{4,5},{5,6},{6,7},{8,9},{9,10},{10,11},{12,13},{... | collective-permute-start | bytes 1486856 | tf_op jit(solution)/shard_map/ppermute | solution.py:324
  72.9 7.3 %collective-permute-done.3 = f32[968,128]{1,0:T(8,128)S(1)} collective-permute-done((f32[968,128]{1,0:T(8,128)S(1)}, f32[968,128]{1,0:T(8,128)S(1)}, u32[]{:S(2)}, u32[]{:S(2)}) %collective-permute-start.3) | collective-permute-done | bytes 495648 | tf_op jit(solution)/shard_map/ppermute | solution.py:325
  80.2 4.4 %collective-permute-done.2 = f32[968,128]{1,0:T(8,128)S(1)} collective-permute-done((f32[968,128]{1,0:T(8,128)S(1)}, f32[968,128]{1,0:T(8,128)S(1)}, u32[]{:S(2)}, u32[]{:S(2)}) %collective-permute-start.2) | collective-permute-done | bytes 495648 | tf_op jit(solution)/shard_map/ppermute | solution.py:324
  84.6 0.1 multiply_add_fusion.packed_ref
  84.7 0.0 copy-done.2
  84.7 36.6 %solves.1 = (f32[1,4096]{1,0:T(1,128)}, f32[1,4096]{1,0:T(1,128)}, f32[1,4096]{1,0:T(1,128)}) custom-call(f32[968,128]{1,0:T(8,128)S(1)} %multiply_add_fusion.packed_ref, bf16[432,4096]{1,0:T(8,128)(2,1)S(1)} %bitcast.9, s32[1,4096]{1,0:T(1,128)S(1)} %bitcast.11, f32[1,4096]{1,0:T(1,128)S(1)} %bitcast.13), custom_call_target="tpu_custom_call" | custom-call | tf_op jit(solution)/shard_map/solves/pallas_call | solution.py:303
Async XLA Ops:
  0.6 4.2 %copy-start = (s32[1,1,4096]{2,1,0:T(1,128)S(1)}, s32[1,1,4096]{2,1,0:T(1,128)}, u32[]{:S(2)}) copy-start(s32[1,1,4096]{2,1,0:T(1,128)} %param.6) | copy-start | bytes 49156
  0.6 45.8 %all-to-all-start = ((bf16[1,2,216,4096]{3,2,0,1:T(8,128)(2,1)}), bf16[1,2,216,4096]{3,2,0,1:T(8,128)(2,1)S(1)}, u32[]{:S(2)}, u32[]{:S(2)}) async-start(bf16[1,2,216,4096]{3,2,0,1:T(8,128)(2,1)} %bitcast.15), calls=%async_computation | async-start | bytes 7077888 | tf_op jit(solution)/shard_map/all_to_all | solution.py:330
  4.9 0.7 copy-start.1
  5.6 0.7 copy-start.7
  6.8 0.6 copy-start.3
  7.4 0.6 copy-start.5
  46.4 0.7 copy-start.4
  47.1 0.7 copy-start.6
  47.8 36.9 %copy-start.2 = (f32[1,1,4096]{2,1,0:T(1,128)S(1)}, f32[1,1,4096]{2,1,0:T(1,128)}, u32[]{:S(2)}) copy-start(f32[1,1,4096]{2,1,0:T(1,128)} %param.7) | copy-start | bytes 49156
  51.4 14.4 %collective-permute-start.1 = (f32[968,128]{1,0:T(8,128)S(1)}, f32[968,128]{1,0:T(8,128)S(1)}, u32[]{:S(2)}, u32[]{:S(2)}) collective-permute-start(f32[968,128]{1,0:T(8,128)S(1)} %grams.1), channel_id=1, source_target_pairs={{4,0},{8,4},{12,8},{5,1},{9,5},{13,9},{6,2},{10,6},{14,10},{7,3},{... | collective-permute-start | bytes 1486856 | tf_op jit(solution)/shard_map/ppermute | solution.py:325
  52.7 14.3 %collective-permute-start = (f32[968,128]{1,0:T(8,128)S(1)}, f32[968,128]{1,0:T(8,128)S(1)}, u32[]{:S(2)}, u32[]{:S(2)}) collective-permute-start(f32[968,128]{1,0:T(8,128)S(1)} %grams.1), channel_id=1, source_target_pairs={{0,4},{4,8},{8,12},{1,5},{5,9},{9,13},{2,6},{6,10},{10,14},{3,7},{... | collective-permute-start | bytes 1486856 | tf_op jit(solution)/shard_map/ppermute | solution.py:324
  67.0 13.2 %collective-permute-start.3 = (f32[968,128]{1,0:T(8,128)S(1)}, f32[968,128]{1,0:T(8,128)S(1)}, u32[]{:S(2)}, u32[]{:S(2)}) collective-permute-start(f32[968,128]{1,0:T(8,128)S(1)} %multiply_add_fusion.1), channel_id=1, source_target_pairs={{1,0},{2,1},{3,2},{5,4},{6,5},{7,6},{9,8},{10,9},{11,10},{13,12},{... | collective-permute-start | bytes 1486856 | tf_op jit(solution)/shard_map/ppermute | solution.py:325
  68.3 16.3 %collective-permute-start.2 = (f32[968,128]{1,0:T(8,128)S(1)}, f32[968,128]{1,0:T(8,128)S(1)}, u32[]{:S(2)}, u32[]{:S(2)}) collective-permute-start(f32[968,128]{1,0:T(8,128)S(1)} %multiply_add_fusion.1), channel_id=1, source_target_pairs={{0,1},{1,2},{2,3},{4,5},{5,6},{6,7},{8,9},{9,10},{10,11},{12,13},{... | collective-permute-start | bytes 1486856 | tf_op jit(solution)/shard_map/ppermute | solution.py:324
where the time goes:
time: 124 us; the launch traced here: 121 us
  waiting for transfers between devices  59.8 us (48%)
  Pallas kernels  40.6 us (33%)
  starting transfers between devices  16 us (13%)
  local copies, waits for them, and re-layouts  4.09 us (3%)
    all_to_all x1, waiting for transfers between devices, on_device(): lax.all_to_all(imagery, 'dates', split_axis=1, concat_axis=2, tiled=True)  38.4 us
    pallas_call x1, Pallas kernels, solves(): pl.pallas_call(solve_kernel, out_shape=(shape, shape, jax.ShapeDtypeStruc...  36.6 us
    ppermute x2, waiting for transfers between devices, window(): after = lax.ppermute(x, axis, down)  15.8 us
    ppermute x2, starting transfers between devices, window(): before = lax.ppermute(x, axis, up)  9.15 us
    ppermute x2, waiting for transfers between devices, window(): before = lax.ppermute(x, axis, up)  5.59 us
    all_to_all x1, starting transfers between devices, on_device(): lax.all_to_all(imagery, 'dates', split_axis=1, concat_axis=2, tiled=True)  4.22 us
    unnamed x16, local copies, waits for them, and re-layouts  4.09 us
    pallas_call x1, Pallas kernels, grams(): pl.pallas_call(gram_kernel, out_shape=jax.ShapeDtypeStruct((rows, LANES),...  3.52 us
  transfers between devices with their start and end apart: 5, of which 5 were waited for; matrix products, arithmetic and copies ran while one was open for 0% of the time, Pallas kernels for 0%

commit v1 on v0

--- a/solution.py
+++ b/solution.py
@@ -1,3 +1,5 @@
+import functools
+
 import jax
 import jax.numpy as jnp
 from jax import lax
@@ -8,6 +10,7 @@
 ridge_term = 0.05
 LANES = 128
 CHUNK = 512
+PIECES = 4
 F32 = jnp.float32
 BF16 = jnp.bfloat16
 NT = (((1,), (1,)), ((), ()))
@@ -315,15 +318,105 @@
     )(packed, feats, index, yields)
 
 
-def window(x, axis):
-    devices = 1
-    for name in axis if isinstance(axis, tuple) else (axis,):
-        devices *= lax.axis_size(name)
-    up = [(i, i + 1) for i in range(devices - 1)]
-    down = [(j, i) for i, j in up]
-    before = lax.ppermute(x, axis, up)
-    after = lax.ppermute(x, axis, down)
-    return 0.5 * before + x + 0.5 * after
+def window_kernel(shape, own_ref, out_ref, landed, middle, send_sem, recv_sem):
+    tiles, cols, dates = shape
+    row = lax.axis_index("tiles")
+    col = lax.axis_index("cols") * dates + lax.axis_index("dates")
+    total = own_ref.shape[0]
+    step = -(-total // (8 * PIECES)) * 8
+    pieces = [pl.ds(at, min(step, total - at)) for at in range(0, total, step)]
+
+    def place(c):
+        return {"cols": c // dates, "dates": c % dates}
+
+    links = (
+        (row < tiles - 1, lambda: {"tiles": row + 1}, row > 0, lambda: {"tiles": row - 1}),
+        (row > 0, lambda: {"tiles": row - 1}, row < tiles - 1, lambda: {"tiles": row + 1}),
+        (col < cols * dates - 1, lambda: place(col + 1), col > 0, lambda: place(col - 1)),
+        (col > 0, lambda: place(col - 1), col < cols * dates - 1, lambda: place(col + 1)),
+    )
+
+    def copy(d, i, source, device):
+        return pltpu.make_async_remote_copy(
+            src_ref=source.at[pieces[i]],
+            dst_ref=landed.at[d, pieces[i]],
+            send_sem=send_sem.at[d, i],
+            recv_sem=recv_sem.at[d, i],
+            device_id=device,
+            device_id_type=pl.DeviceIdType.MESH,
+        )
+
+    barrier = pltpu.get_barrier_semaphore()
+    for there, target, _, _ in links:
+
+        @pl.when(there)
+        def _(target=target):
+            pl.semaphore_signal(
+                barrier, inc=1, device_id=target(), device_id_type=pl.DeviceIdType.MESH
+            )
+
+    peers = sum(there.astype(jnp.int32) for there, _, _, _ in links)
+    pl.semaphore_wait(barrier, peers)
+
+    def send(d, i, source):
+        there, target, _, _ = links[d]
+
+        @pl.when(there)
+        def _():
+            copy(d, i, source, target()).start()
+
+    def receive(d, i, source, into):
+        _, _, there, origin = links[d]
+
+        @pl.when(there)
+        def _():
+            copy(d, i, source, origin()).wait_recv()
+            into[pieces[i]] += 0.5 * landed[d, pieces[i]]
+
+    count = len(pieces)
+    for i in range(count):
+        send(0, i, own_ref)
+        send(1, i, own_ref)
+    for i in range(count):
+        middle[pieces[i]] = own_ref[pieces[i]]
+        receive(0, i, own_ref, middle)
+        receive(1, i, own_ref, middle)
+        send(2, i, middle)
+        send(3, i, middle)
+    for i in range(count):
+        out_ref[pieces[i]] = middle[pieces[i]]
+        receive(2, i, middle, out_ref)
+        receive(3, i, middle, out_ref)
+    for i in range(count):
+        for d in range(4):
+            there, target, _, _ = links[d]
+
+            @pl.when(there)
+            def _(d=d, i=i, target=target):
+                copy(d, i, own_ref if d < 2 else middle, target()).wait_send()
+
+
+def window(packed):
+    shape = tuple(lax.axis_size(name) for name in ("tiles", "cols", "dates"))
+    in_vmem = pl.BlockSpec(memory_space=pltpu.VMEM)
+    return pl.pallas_call(
+        functools.partial(window_kernel, shape),
+        out_shape=jax.ShapeDtypeStruct(packed.shape, F32),
+        in_specs=[in_vmem],
+        out_specs=in_vmem,
+        scratch_shapes=[
+            pltpu.VMEM((4,) + packed.shape, F32),
+            pltpu.VMEM(packed.shape, F32),
+            pltpu.SemaphoreType.DMA((4, PIECES)),
+            pltpu.SemaphoreType.DMA((4, PIECES)),
+        ],
+        compiler_params=pltpu.CompilerParams(
+            collective_id=0,
+            has_side_effects=True,
+            vmem_limit_bytes=48 * 1024 * 1024,
+        ),
+        name="window",
+    )(packed)
 
 
 def on_device(imagery, pixel_mask, point_pixel, point_yield):
@@ -335,8 +428,7 @@
     mask = pixel_mask.reshape(pixels // LANES, LANES)
     weight, product = segments(index, yields, mask)
     packed = grams(feats, weight, product)
-    packed = window(packed, "tiles")
-    packed = window(packed, ("cols", "dates"))
+    packed = window(packed)
     fitted, spread, resid = solves(packed, feats, index, yields)
     return (fitted[None], spread[None], resid[None])
 

time: 124 us -> 112 us (0.903); the launches traced: 121 us -> 111 us
  Pallas kernels: 40.6 us -> 64 us
  waiting for transfers between devices: 59.8 us -> 38.4 us
  starting transfers between devices: 16 us -> 4.22 us
    pallas_call x0 -> x1, Pallas kernels: none -> 23.3 us  [window(): pl.pallas_call(functools.partial(window_kernel, shape), out_shape=jax.Sha...]
    ppermute x4 -> x0, waiting for transfers between devices: 21.4 us -> none  [the longest x2 15.8 us: window(): after = lax.ppermute(x, axis, down)]
    ppermute x4 -> x0, starting transfers between devices: 11.7 us -> none  [the longest x2 9.15 us: window(): before = lax.ppermute(x, axis, up)]
  transfers between devices with their start and end apart: 5 -> 1, of which waited for: 5 -> 1; matrix products, arithmetic and copies ran while one was open for 0% -> 0% of each run, Pallas kernels for 0% -> 0%
where the time goes in v1:
time: 112 us; the launch traced here: 111 us
  Pallas kernels  64 us (57%)
  waiting for transfers between devices  38.4 us (34%)
  starting transfers between devices  4.22 us (4%)
  local copies, waits for them, and re-layouts  4.1 us (4%)
    all_to_all x1, waiting for transfers between devices, on_device(): lax.all_to_all(imagery, 'dates', split_axis=1, concat_axis=2, tiled=True)  38.4 us
    pallas_call x1, Pallas kernels, solves(): pl.pallas_call(solve_kernel, out_shape=(shape, shape, jax.ShapeDtypeStruc...  36.7 us
    pallas_call x1, Pallas kernels, window(): pl.pallas_call(functools.partial(window_kernel, shape), out_shape=jax.Sha...  23.3 us
    all_to_all x1, starting transfers between devices, on_device(): lax.all_to_all(imagery, 'dates', split_axis=1, concat_axis=2, tiled=True)  4.22 us
    unnamed x16, local copies, waits for them, and re-layouts  4.1 us
    pallas_call x1, Pallas kernels, grams(): pl.pallas_call(gram_kernel, out_shape=jax.ShapeDtypeStruct((rows, LANES),...  3.52 us
  transfers between devices with their start and end apart: 1, of which 1 were waited for; matrix products, arithmetic and copies ran while one was open for 0% of the time, Pallas kernels for 0%

profile of v1, /device:TPU:0, one launch (start us, length us, event | category | flops | bytes accessed | tf_op | source)
XLA Modules:
  0.0 111.4 jit_solution(14365116879069133571)
XLA Ops:
  0.6 0.0 copy-start
  0.6 4.2 %all-to-all-start = ((bf16[1,2,216,4096]{3,2,0,1:T(8,128)(2,1)}), bf16[1,2,216,4096]{3,2,0,1:T(8,128)(2,1)S(1)}, u32[]{:S(2)}, u32[]{:S(2)}) async-start(bf16[1,2,216,4096]{3,2,0,1:T(8,128)(2,1)} %bitcast.15), calls=%async_computation | async-start | bytes 7077888 | tf_op jit(solution)/shard_map/all_to_all | solution.py:423
  4.9 0.0 copy-done
  4.9 0.0 copy-start.1
  4.9 0.7 copy-done.1
  5.6 0.0 copy-start.7
  5.6 0.7 copy-done.7
  6.3 0.5 segments.1
  6.8 0.0 copy-start.3
  6.8 0.6 copy-done.3
  7.4 0.0 copy-start.5
  7.4 0.6 copy-done.5
  8.0 38.4 %all-to-all-done = bf16[1,2,216,4096]{3,2,0,1:T(8,128)(2,1)S(1)} async-done(((bf16[1,2,216,4096]{3,2,0,1:T(8,128)(2,1)}), bf16[1,2,216,4096]{3,2,0,1:T(8,128)(2,1)S(1)}, u32[]{:S(2)}, u32[]{:S(2)}) %all-to-all-start) | async-done | bytes 3538976 | tf_op jit(solution)/shard_map/all_to_all | solution.py:423
  46.4 0.0 copy-start.2
  46.4 0.0 copy-start.4
  46.4 0.7 copy-done.4
  47.1 0.0 copy-start.6
  47.1 0.7 copy-done.6
  47.9 3.5 %grams.1.own_ref = f32[968,128]{1,0:T(8,128)S(1)} custom-call(bf16[432,4096]{1,0:T(8,128)(2,1)S(1)} %bitcast.8, f32[32,128]{1,0:T(8,128)S(1)} %copy-done.4, f32[32,128]{1,0:T(8,128)S(1)} %copy-done.6), custom_call_target="tpu_custom_call" | custom-call | tf_op jit(solution)/shard_map/grams/pallas_call | solution.py:293
  51.4 23.3 %window.1.packed_ref = f32[968,128]{1,0:T(8,128)S(1)} custom-call(f32[968,128]{1,0:T(8,128)S(1)} %grams.1.own_ref), custom_call_target="tpu_custom_call" | custom-call | tf_op jit(solution)/shard_map/window/pallas_call | solution.py:402
  74.7 0.0 copy-done.2
  74.7 36.7 %solves.1 = (f32[1,4096]{1,0:T(1,128)}, f32[1,4096]{1,0:T(1,128)}, f32[1,4096]{1,0:T(1,128)}) custom-call(f32[968,128]{1,0:T(8,128)S(1)} %window.1.packed_ref, bf16[432,4096]{1,0:T(8,128)(2,1)S(1)} %bitcast.9, s32[1,4096]{1,0:T(1,128)S(1)} %bitcast.11, f32[1,4096]{1,0:T(1,128)S(1)} %bitcast.13), custom_call_target="tpu_custom_call" | custom-call | tf_op jit(solution)/shard_map/solves/pallas_call | solution.py:306
Async XLA Ops:
  0.6 4.2 %copy-start = (s32[1,1,4096]{2,1,0:T(1,128)S(1)}, s32[1,1,4096]{2,1,0:T(1,128)}, u32[]{:S(2)}) copy-start(s32[1,1,4096]{2,1,0:T(1,128)} %param.6) | copy-start | bytes 49156
  0.6 45.8 %all-to-all-start = ((bf16[1,2,216,4096]{3,2,0,1:T(8,128)(2,1)}), bf16[1,2,216,4096]{3,2,0,1:T(8,128)(2,1)S(1)}, u32[]{:S(2)}, u32[]{:S(2)}) async-start(bf16[1,2,216,4096]{3,2,0,1:T(8,128)(2,1)} %bitcast.15), calls=%async_computation | async-start | bytes 7077888 | tf_op jit(solution)/shard_map/all_to_all | solution.py:423
  4.9 0.7 copy-start.1
  5.6 0.7 copy-start.7
  6.8 0.6 copy-start.3
  7.4 0.6 copy-start.5
  46.4 28.3 %copy-start.2 = (f32[1,1,4096]{2,1,0:T(1,128)S(1)}, f32[1,1,4096]{2,1,0:T(1,128)}, u32[]{:S(2)}) copy-start(f32[1,1,4096]{2,1,0:T(1,128)} %param.7) | copy-start | bytes 49156
  46.4 0.7 copy-start.4
  47.1 0.7 copy-start.6

commit v2 on v1

--- a/solution.py
+++ b/solution.py
@@ -10,7 +10,7 @@
 ridge_term = 0.05
 LANES = 128
 CHUNK = 512
-PIECES = 4
+PIECES = 8
 F32 = jnp.float32
 BF16 = jnp.bfloat16
 NT = (((1,), (1,)), ((), ()))

time: 112 us -> 111 us (level)
  no operation moved by 1% of the time
where the time goes in v2:
time: 111 us
  Pallas kernels  63.3 us (57%)
  waiting for transfers between devices  38.4 us (35%)
  starting transfers between devices  4.22 us (4%)
  local copies, waits for them, and re-layouts  4.1 us (4%)
    all_to_all x1, waiting for transfers between devices, on_device(): lax.all_to_all(imagery, 'dates', split_axis=1, concat_axis=2, tiled=True)  38.4 us
    pallas_call x1, Pallas kernels, solves(): pl.pallas_call(solve_kernel, out_shape=(shape, shape, jax.ShapeDtypeStruc...  36.6 us
    pallas_call x1, Pallas kernels, window(): pl.pallas_call(functools.partial(window_kernel, shape), out_shape=jax.Sha...  22.7 us
    all_to_all x1, starting transfers between devices, on_device(): lax.all_to_all(imagery, 'dates', split_axis=1, concat_axis=2, tiled=True)  4.22 us
    unnamed x16, local copies, waits for them, and re-layouts  4.1 us
    pallas_call x1, Pallas kernels, grams(): pl.pallas_call(gram_kernel, out_shape=jax.ShapeDtypeStruct((rows, LANES),...  3.52 us
  transfers between devices with their start and end apart: 1, of which 1 were waited for; matrix products, arithmetic and copies ran while one was open for 0% of the time, Pallas kernels for 0%

profile of v2, /device:TPU:0, one launch (start us, length us, event | category | flops | bytes accessed | tf_op | source)
XLA Modules:
  0.0 110.7 jit_solution(14795267165559050753)
XLA Ops:
  0.6 0.0 copy-start
  0.6 4.2 %all-to-all-start = ((bf16[1,2,216,4096]{3,2,0,1:T(8,128)(2,1)}), bf16[1,2,216,4096]{3,2,0,1:T(8,128)(2,1)S(1)}, u32[]{:S(2)}, u32[]{:S(2)}) async-start(bf16[1,2,216,4096]{3,2,0,1:T(8,128)(2,1)} %bitcast.15), calls=%async_computation | async-start | bytes 7077888 | tf_op jit(solution)/shard_map/all_to_all | solution.py:423
  4.9 0.0 copy-done
  4.9 0.0 copy-start.1
  4.9 0.7 copy-done.1
  5.6 0.0 copy-start.7
  5.6 0.7 copy-done.7
  6.3 0.5 segments.1
  6.8 0.0 copy-start.3
  6.8 0.6 copy-done.3
  7.4 0.0 copy-start.5
  7.4 0.6 copy-done.5
  8.0 38.4 %all-to-all-done = bf16[1,2,216,4096]{3,2,0,1:T(8,128)(2,1)S(1)} async-done(((bf16[1,2,216,4096]{3,2,0,1:T(8,128)(2,1)}), bf16[1,2,216,4096]{3,2,0,1:T(8,128)(2,1)S(1)}, u32[]{:S(2)}, u32[]{:S(2)}) %all-to-all-start) | async-done | bytes 3538976 | tf_op jit(solution)/shard_map/all_to_all | solution.py:423
  46.4 0.0 copy-start.2
  46.4 0.0 copy-start.4
  46.4 0.7 copy-done.4
  47.1 0.0 copy-start.6
  47.1 0.7 copy-done.6
  47.9 3.5 %grams.1.own_ref = f32[968,128]{1,0:T(8,128)S(1)} custom-call(bf16[432,4096]{1,0:T(8,128)(2,1)S(1)} %bitcast.8, f32[32,128]{1,0:T(8,128)S(1)} %copy-done.4, f32[32,128]{1,0:T(8,128)S(1)} %copy-done.6), custom_call_target="tpu_custom_call" | custom-call | tf_op jit(solution)/shard_map/grams/pallas_call | solution.py:293
  51.4 22.7 %window.1.packed_ref = f32[968,128]{1,0:T(8,128)S(1)} custom-call(f32[968,128]{1,0:T(8,128)S(1)} %grams.1.own_ref), custom_call_target="tpu_custom_call" | custom-call | tf_op jit(solution)/shard_map/window/pallas_call | solution.py:402
  74.1 0.0 copy-done.2
  74.1 36.6 %solves.1 = (f32[1,4096]{1,0:T(1,128)}, f32[1,4096]{1,0:T(1,128)}, f32[1,4096]{1,0:T(1,128)}) custom-call(f32[968,128]{1,0:T(8,128)S(1)} %window.1.packed_ref, bf16[432,4096]{1,0:T(8,128)(2,1)S(1)} %bitcast.9, s32[1,4096]{1,0:T(1,128)S(1)} %bitcast.11, f32[1,4096]{1,0:T(1,128)S(1)} %bitcast.13), custom_call_target="tpu_custom_call" | custom-call | tf_op jit(solution)/shard_map/solves/pallas_call | solution.py:306
Async XLA Ops:
  0.6 4.2 %copy-start = (s32[1,1,4096]{2,1,0:T(1,128)S(1)}, s32[1,1,4096]{2,1,0:T(1,128)}, u32[]{:S(2)}) copy-start(s32[1,1,4096]{2,1,0:T(1,128)} %param.6) | copy-start | bytes 49156
  0.6 45.8 %all-to-all-start = ((bf16[1,2,216,4096]{3,2,0,1:T(8,128)(2,1)}), bf16[1,2,216,4096]{3,2,0,1:T(8,128)(2,1)S(1)}, u32[]{:S(2)}, u32[]{:S(2)}) async-start(bf16[1,2,216,4096]{3,2,0,1:T(8,128)(2,1)} %bitcast.15), calls=%async_computation | async-start | bytes 7077888 | tf_op jit(solution)/shard_map/all_to_all | solution.py:423
  4.9 0.7 copy-start.1
  5.6 0.7 copy-start.7
  6.8 0.6 copy-start.3
  7.4 0.6 copy-start.5
  46.4 27.7 %copy-start.2 = (f32[1,1,4096]{2,1,0:T(1,128)S(1)}, f32[1,1,4096]{2,1,0:T(1,128)}, u32[]{:S(2)}) copy-start(f32[1,1,4096]{2,1,0:T(1,128)} %param.7) | copy-start | bytes 49156
  46.4 0.7 copy-start.4
  47.1 0.7 copy-start.6

commit v3 on v2

--- a/solution.py
+++ b/solution.py
@@ -118,7 +118,7 @@
     return p
 
 
-def block_inverse(block, pivots, group=4):
+def block_inverse(block, pivots, group=8):
     tiles = [block[8 * g : 8 * g + 8] for g in range(LANES // 8)]
     lane = lax.broadcasted_iota(jnp.int32, (8, LANES), 1)
     line = lax.broadcasted_iota(jnp.int32, (8, LANES), 0)

time: 111 us -> 107 us (0.964)
  Pallas kernels: 63.3 us -> 58.6 us
    pallas_call x1, Pallas kernels: 36.6 us -> 31.9 us  [solves(): pl.pallas_call(solve_kernel, out_shape=(shape, shape, jax.ShapeDtypeStruc...]
where the time goes in v3:
time: 107 us; the launch traced here: 106 us
  Pallas kernels  58.6 us (55%)
  waiting for transfers between devices  38.4 us (36%)
  starting transfers between devices  4.22 us (4%)
  local copies, waits for them, and re-layouts  4.1 us (4%)
    all_to_all x1, waiting for transfers between devices, on_device(): lax.all_to_all(imagery, 'dates', split_axis=1, concat_axis=2, tiled=True)  38.4 us
    pallas_call x1, Pallas kernels, solves(): pl.pallas_call(solve_kernel, out_shape=(shape, shape, jax.ShapeDtypeStruc...  31.9 us
    pallas_call x1, Pallas kernels, window(): pl.pallas_call(functools.partial(window_kernel, shape), out_shape=jax.Sha...  22.7 us
    all_to_all x1, starting transfers between devices, on_device(): lax.all_to_all(imagery, 'dates', split_axis=1, concat_axis=2, tiled=True)  4.22 us
    unnamed x16, local copies, waits for them, and re-layouts  4.1 us
    pallas_call x1, Pallas kernels, grams(): pl.pallas_call(gram_kernel, out_shape=jax.ShapeDtypeStruct((rows, LANES),...  3.52 us
  transfers between devices with their start and end apart: 1, of which 1 were waited for; matrix products, arithmetic and copies ran while one was open for 0% of the time, Pallas kernels for 0%

profile of v3, /device:TPU:0, one launch (start us, length us, event | category | flops | bytes accessed | tf_op | source)
XLA Modules:
  0.0 106.0 jit_solution(14838098726281168763)
XLA Ops:
  0.6 0.0 copy-start
  0.6 4.2 %all-to-all-start = ((bf16[1,2,216,4096]{3,2,0,1:T(8,128)(2,1)}), bf16[1,2,216,4096]{3,2,0,1:T(8,128)(2,1)S(1)}, u32[]{:S(2)}, u32[]{:S(2)}) async-start(bf16[1,2,216,4096]{3,2,0,1:T(8,128)(2,1)} %bitcast.15), calls=%async_computation | async-start | bytes 7077888 | tf_op jit(solution)/shard_map/all_to_all | solution.py:423
  4.9 0.0 copy-done
  4.9 0.0 copy-start.1
  4.9 0.7 copy-done.1
  5.6 0.0 copy-start.7
  5.6 0.7 copy-done.7
  6.3 0.5 segments.1
  6.8 0.0 copy-start.3
  6.8 0.6 copy-done.3
  7.4 0.0 copy-start.5
  7.4 0.6 copy-done.5
  8.0 38.4 %all-to-all-done = bf16[1,2,216,4096]{3,2,0,1:T(8,128)(2,1)S(1)} async-done(((bf16[1,2,216,4096]{3,2,0,1:T(8,128)(2,1)}), bf16[1,2,216,4096]{3,2,0,1:T(8,128)(2,1)S(1)}, u32[]{:S(2)}, u32[]{:S(2)}) %all-to-all-start) | async-done | bytes 3538976 | tf_op jit(solution)/shard_map/all_to_all | solution.py:423
  46.4 0.0 copy-start.2
  46.4 0.0 copy-start.4
  46.4 0.7 copy-done.4
  47.1 0.0 copy-start.6
  47.1 0.7 copy-done.6
  47.9 3.5 %grams.1.own_ref = f32[968,128]{1,0:T(8,128)S(1)} custom-call(bf16[432,4096]{1,0:T(8,128)(2,1)S(1)} %bitcast.8, f32[32,128]{1,0:T(8,128)S(1)} %copy-done.4, f32[32,128]{1,0:T(8,128)S(1)} %copy-done.6), custom_call_target="tpu_custom_call" | custom-call | tf_op jit(solution)/shard_map/grams/pallas_call | solution.py:293
  51.4 22.7 %window.1.packed_ref = f32[968,128]{1,0:T(8,128)S(1)} custom-call(f32[968,128]{1,0:T(8,128)S(1)} %grams.1.own_ref), custom_call_target="tpu_custom_call" | custom-call | tf_op jit(solution)/shard_map/window/pallas_call | solution.py:402
  74.1 0.0 copy-done.2
  74.1 31.9 %solves.1 = (f32[1,4096]{1,0:T(1,128)}, f32[1,4096]{1,0:T(1,128)}, f32[1,4096]{1,0:T(1,128)}) custom-call(f32[968,128]{1,0:T(8,128)S(1)} %window.1.packed_ref, bf16[432,4096]{1,0:T(8,128)(2,1)S(1)} %bitcast.9, s32[1,4096]{1,0:T(1,128)S(1)} %bitcast.11, f32[1,4096]{1,0:T(1,128)S(1)} %bitcast.13), custom_call_target="tpu_custom_call" | custom-call | tf_op jit(solution)/shard_map/solves/pallas_call | solution.py:306
Async XLA Ops:
  0.6 4.2 %copy-start = (s32[1,1,4096]{2,1,0:T(1,128)S(1)}, s32[1,1,4096]{2,1,0:T(1,128)}, u32[]{:S(2)}) copy-start(s32[1,1,4096]{2,1,0:T(1,128)} %param.6) | copy-start | bytes 49156
  0.6 45.8 %all-to-all-start = ((bf16[1,2,216,4096]{3,2,0,1:T(8,128)(2,1)}), bf16[1,2,216,4096]{3,2,0,1:T(8,128)(2,1)S(1)}, u32[]{:S(2)}, u32[]{:S(2)}) async-start(bf16[1,2,216,4096]{3,2,0,1:T(8,128)(2,1)} %bitcast.15), calls=%async_computation | async-start | bytes 7077888 | tf_op jit(solution)/shard_map/all_to_all | solution.py:423
  4.9 0.7 copy-start.1
  5.6 0.7 copy-start.7
  6.8 0.6 copy-start.3
  7.4 0.6 copy-start.5
  46.4 27.7 %copy-start.2 = (f32[1,1,4096]{2,1,0:T(1,128)S(1)}, f32[1,1,4096]{2,1,0:T(1,128)}, u32[]{:S(2)}) copy-start(f32[1,1,4096]{2,1,0:T(1,128)} %param.7) | copy-start | bytes 49156
  46.4 0.7 copy-start.4
  47.1 0.7 copy-start.6
